TPU v7x, 256 devices: a whole 4x4x8 slice. The times are simulated.
256 devices in a mesh: seq: 32 (over z, x), doc: 8 (over y, core).
Axes of the slice: x: 4, y: 4, z: 8, core: 2. Of those that a mesh axis runs over, the one named last changes fastest.
Arguments:
- queries: bfloat16 [24576, 4096], P(('doc', 'seq')), parts along dimension 0, may hold values from -250 to 250
- keys: bfloat16 [24576, 4096], P(('doc', 'seq')), parts along dimension 0, may hold values from -13 to 13
- values: bfloat16 [24576, 4096], P(('doc', 'seq')), parts along dimension 0, may hold values from -6 to 6
- fresh_queries: bfloat16 [24576, 4096], P(('doc', 'seq')), parts along dimension 0, may hold values from -250 to 250
- fresh_keys: bfloat16 [24576, 4096], P(('doc', 'seq')), parts along dimension 0, may hold values from -6 to 6
- fresh_values: bfloat16 [24576, 4096], P(('doc', 'seq')), parts along dimension 0, may hold values from -6 to 6
- masked_rows: int32 [256, 48], P(('doc', 'seq')), parts along dimension 0, may hold values from 0 to 95, as said below
- masked_counts: int32 [256], P(('doc', 'seq')), parts along dimension 0, may hold values from 1 to 48, as said below
Outputs:
- refresh_out: bfloat16 [24576, 4096], P(('doc', 'seq')), parts along dimension 0
- cached_out: bfloat16 [12288, 4096], P(('doc', 'seq')), parts along dimension 0
There are 8 independent parts, one for each index of `doc`. A program takes and returns all parts, laid end to end along the dimension named above; each array names one. Nothing has to cross between parts.
Inputs may be any that keep to these rules, and one draw needn't show every extreme that they name: `masked_rows`: each shard's 48 entries are different positions of that shard; only the first masked_counts of them are still masked, the rest are ignored. `masked_counts`: some shard has all 48 slots live in every draw.
All inputs are finite; a program needn't handle non-finite values.
Results may differ from a plain program's by a relative error of at most 0.005.
Values may be sent and summed in bfloat16 or wider, within the bound.
A program may use at most 64 MiB of HBM per device.

v0:
```python
import math

import jax
import jax.numpy as jnp
from jax import lax
from jax.sharding import PartitionSpec as P

HEAD_DIM = 128


def attend(query_rows, key_rows, value_rows):
    row_total, width_cols = query_rows.shape
    head_count = width_cols // HEAD_DIM
    block_rows = min(512, row_total)
    score_scale = 1.0 / math.sqrt(HEAD_DIM)
    key_heads = key_rows.reshape(-1, head_count, HEAD_DIM)
    value_heads = value_rows.reshape(-1, head_count, HEAD_DIM)
    blocks_in = query_rows.reshape(row_total // block_rows, block_rows, head_count, HEAD_DIM)

    def one_block(query_block):
        scores = (
            jnp.einsum("qhd,khd->hqk", query_block, key_heads, preferred_element_type=jnp.float32)
            * score_scale
        )
        row_top = jnp.max(scores, axis=-1, keepdims=True)
        powers = jnp.exp(scores - row_top)
        weights = (powers / jnp.sum(powers, axis=-1, keepdims=True)).astype(jnp.bfloat16)
        mixed = jnp.einsum("hqk,khd->qhd", weights, value_heads, preferred_element_type=jnp.float32)
        return mixed.astype(jnp.bfloat16).reshape(block_rows, width_cols)

    return lax.map(one_block, blocks_in).reshape(row_total, width_cols)


def per_device(
    queries, keys, values, fresh_queries, fresh_keys, fresh_values, masked_rows, masked_counts
):
    own_rows = queries.shape[0]
    slot_count = masked_rows.shape[1]
    shards = lax.axis_size("seq")
    outgoing = (fresh_queries, fresh_keys, fresh_values)
    head_queries, head_keys, head_values = (
        lax.all_to_all(queries, "seq", split_axis=1, concat_axis=0, tiled=True),
        lax.all_to_all(keys, "seq", split_axis=1, concat_axis=0, tiled=True),
        lax.all_to_all(values, "seq", split_axis=1, concat_axis=0, tiled=True),
    )
    new_queries, new_keys, new_values = (
        lax.all_to_all(outgoing[0], "seq", split_axis=1, concat_axis=0, tiled=True),
        lax.all_to_all(outgoing[1], "seq", split_axis=1, concat_axis=0, tiled=True),
        lax.all_to_all(outgoing[2], "seq", split_axis=1, concat_axis=0, tiled=True),
    )
    slot_lists, counts = (
        lax.all_gather(masked_rows, "seq", axis=0, tiled=True),
        lax.all_gather(masked_counts, "seq", axis=0, tiled=True),
    )
    shard_ids = jnp.arange(shards, dtype=jnp.int32)
    positions = (shard_ids[:, None] * own_rows + slot_lists).reshape(-1)
    live_slots = (jnp.arange(slot_count, dtype=jnp.int32)[None, :] < counts[:, None]).reshape(-1)
    new_queries = new_queries[positions]
    new_keys = new_keys[positions]
    new_values = new_values[positions]
    target = jnp.where(live_slots, positions, shards * own_rows)
    cache_keys = head_keys.at[target].set(new_keys, mode="drop")
    cache_values = head_values.at[target].set(new_values, mode="drop")
    refresh_heads = attend(head_queries, head_keys, head_values)
    cached_heads = jnp.where(
        live_slots[:, None],
        attend(new_queries, cache_keys, cache_values),
        jnp.zeros((), jnp.bfloat16),
    )
    refresh_out = lax.all_to_all(refresh_heads, "seq", split_axis=0, concat_axis=1, tiled=True)
    cached_out = lax.all_to_all(cached_heads, "seq", split_axis=0, concat_axis=1, tiled=True)
    return (refresh_out, cached_out)


def solution(mesh):
    in_specs = (
        P(("doc", "seq"), None),
        P(("doc", "seq"), None),
        P(("doc", "seq"), None),
        P(("doc", "seq"), None),
        P(("doc", "seq"), None),
        P(("doc", "seq"), None),
        P(("doc", "seq"), None),
        P(("doc", "seq")),
    )
    out_specs = (P(("doc", "seq"), None), P(("doc", "seq"), None))
    return jax.shard_map(
        per_device, mesh=mesh, in_specs=in_specs, out_specs=out_specs, check_vma=False
    )
```

profile of v0, /device:TPU:62, one launch (start us, length us, event | category | flops | bytes accessed | tf_op | source)
XLA Modules:
  0.0 310.3 jit_solution(2706946988286956805)
XLA Ops:
  2.8 11.1 %all-to-all-start.1 = ((bf16[96,32,128]{2,0,1:T(8,128)(2,1)}), bf16[96,32,128]{2,0,1:T(8,128)(2,1)S(1)}, u32[]{:S(2)}, u32[]{:S(2)}) async-start(bf16[96,32,128]{2,0,1:T(8,128)(2,1)} %copy_bitcast_fusion.5), calls=%async_computation.1 | async-start | bytes 1572864 | tf_op jit(solution)/shard_map/all_to_all | solution.py:43
  13.9 2.2 copy_bitcast_fusion.4
  16.1 19.4 %all-to-all-done.1 = bf16[96,32,128]{2,0,1:T(8,128)(2,1)S(1)} async-done(((bf16[96,32,128]{2,0,1:T(8,128)(2,1)}), bf16[96,32,128]{2,0,1:T(8,128)(2,1)S(1)}, u32[]{:S(2)}, u32[]{:S(2)}) %all-to-all-start.1) | async-done | bytes 786464 | tf_op jit(solution)/shard_map/all_to_all | solution.py:43
  35.5 6.4 %all-to-all-start.2 = ((bf16[96,32,128]{2,0,1:T(8,128)(2,1)}), bf16[96,32,128]{2,0,1:T(8,128)(2,1)S(1)}, u32[]{:S(2)}, u32[]{:S(2)}) async-start(bf16[96,32,128]{2,0,1:T(8,128)(2,1)} %copy_bitcast_fusion.4), calls=%async_computation.2 | async-start | bytes 1572864 | tf_op jit(solution)/shard_map/all_to_all | solution.py:44
  42.9 19.4 %all-to-all-done.2 = bf16[96,32,128]{2,0,1:T(8,128)(2,1)S(1)} async-done(((bf16[96,32,128]{2,0,1:T(8,128)(2,1)}), bf16[96,32,128]{2,0,1:T(8,128)(2,1)S(1)}, u32[]{:S(2)}, u32[]{:S(2)}) %all-to-all-start.2) | async-done | bytes 786464 | tf_op jit(solution)/shard_map/all_to_all | solution.py:44
  63.2 6.4 %all-to-all-start.4 = ((bf16[96,32,128]{2,0,1:T(8,128)(2,1)}), bf16[96,32,128]{2,0,1:T(8,128)(2,1)S(1)}, u32[]{:S(2)}, u32[]{:S(2)}) async-start(bf16[96,32,128]{2,0,1:T(8,128)(2,1)} %copy_bitcast_fusion.3), calls=%async_computation.4 | async-start | bytes 1572864 | tf_op jit(solution)/shard_map/all_to_all | solution.py:47
  69.7 2.2 copy_bitcast_fusion.2
  71.9 17.7 %all-to-all-done.4 = bf16[96,32,128]{2,0,1:T(8,128)(2,1)S(1)} async-done(((bf16[96,32,128]{2,0,1:T(8,128)(2,1)}), bf16[96,32,128]{2,0,1:T(8,128)(2,1)S(1)}, u32[]{:S(2)}, u32[]{:S(2)}) %all-to-all-start.4) | async-done | bytes 786464 | tf_op jit(solution)/shard_map/all_to_all | solution.py:47
  89.6 6.5 %all-to-all-start.5 = ((bf16[96,32,128]{2,0,1:T(8,128)(2,1)}), bf16[96,32,128]{2,0,1:T(8,128)(2,1)}, u32[]{:S(2)}, u32[]{:S(2)}) async-start(bf16[96,32,128]{2,0,1:T(8,128)(2,1)} %copy_bitcast_fusion.2), calls=%async_computation.5 | async-start | bytes 1572864 | tf_op jit(solution)/shard_map/all_to_all | solution.py:48
  96.1 2.1 copy_bitcast_fusion.1
  98.2 17.7 %all-to-all-done.5 = bf16[96,32,128]{2,0,1:T(8,128)(2,1)} async-done(((bf16[96,32,128]{2,0,1:T(8,128)(2,1)}), bf16[96,32,128]{2,0,1:T(8,128)(2,1)}, u32[]{:S(2)}, u32[]{:S(2)}) %all-to-all-start.5) | async-done | bytes 786464 | tf_op jit(solution)/shard_map/all_to_all | solution.py:48
  116.0 6.5 %all-to-all-start.6 = ((bf16[96,32,128]{2,0,1:T(8,128)(2,1)}), bf16[96,32,128]{2,0,1:T(8,128)(2,1)}, u32[]{:S(2)}, u32[]{:S(2)}) async-start(bf16[96,32,128]{2,0,1:T(8,128)(2,1)} %copy_bitcast_fusion.1), calls=%async_computation.6 | async-start | bytes 1572864 | tf_op jit(solution)/shard_map/all_to_all | solution.py:49
  124.6 22.0 %all-reduce = s32[32]{0:T(128)S(1)} all-reduce(s32[32]{0:T(128)S(1)} %dynamic-update-slice), channel_id=1, replica_groups=mesh['seq'=32,'doc'=8] {'seq'}, use_global_device_ids=true, to_apply=%add | all-reduce | flops 32 | bytes 256
  146.8 36.5 %all-gather = s32[32,1,48]{2,1,0:T(1,128)S(1)} all-gather(s32[1,1,48]{2,1,0:T(1,128)S(1)} %bitcast.149), channel_id=1, replica_groups=mesh['seq'=32,'doc'=8] {'seq'}, dimensions={0}, use_global_device_ids=true | all-gather | bytes 6336 | tf_op jit(solution)/shard_map/all_gather | solution.py:52
  185.3 2.1 copy.96
  187.4 3.2 %gather_fusion = bf16[1536,128]{1,0:T(8,128)(2,1)S(1)} fusion(bf16[3072,128]{1,0:T(8,128)(2,1)S(1)} %bitcast.141, s32[2048]{0:T(1024)S(1)} %pad_clamp_fusion), kind=kCustom, calls=%fused_computation | custom fusion | bytes 792576 | tf_op jit(solution)/shard_map/gather | solution.py:58
  190.6 14.3 %scatter_custom_fusion = bf16[3072,128]{1,0:T(8,128)(2,1)S(1)} fusion(bf16[3072,128]{1,0:T(8,128)(2,1)S(1)} %copy.95, s32[1536]{0:T(1024)} %get-tuple-element.113, bf16[3072,128]{1,0:T(8,128)(2,1)} %bitcast.32, s32[2048]{0:T(1024)S(1)} %pad_clamp_fusion), kind=kCustom, calls=%fused_computation.45 | custom fusion | bytes 786432 | tf_op jit(solution)/shard_map/scatter | solution.py:62
  204.8 8.3 %all-to-all-start = ((bf16[96,32,128]{2,0,1:T(8,128)(2,1)}), bf16[96,32,128]{2,0,1:T(8,128)(2,1)}, u32[]{:S(2)}, u32[]{:S(2)}) async-start(bf16[96,32,128]{2,0,1:T(8,128)(2,1)} %copy_bitcast_fusion.6), calls=%async_computation | async-start | bytes 1572864 | tf_op jit(solution)/shard_map/all_to_all | solution.py:42
  213.2 16.0 %scatter_custom_fusion.1 = bf16[3072,128]{1,0:T(8,128)(2,1)} fusion(bf16[3072,128]{1,0:T(8,128)(2,1)} %copy.96, s32[1536]{0:T(1024)} %get-tuple-element.113, bf16[3072,128]{1,0:T(8,128)(2,1)} %bitcast.36, s32[2048]{0:T(1024)S(1)} %pad_clamp_fusion), kind=kCustom, calls=%fused_computation.43 | custom fusion | bytes 786432 | tf_op jit(solution)/shard_map/scatter | solution.py:63
  229.1 12.9 %while.21 = (s32[]{:T(128)}, bf16[3,512,128]{2,1,0:T(8,128)(2,1)}, bf16[3,512,1,128]{3,1,2,0:T(8,128)(2,1)S(1)}, bf16[3072,1,128]{2,0,1:T(8,128)(2,1)S(1)}, bf16[3072,1,128]{2,0,1:T(8,128)(2,1)}, /*index=5*/s32[]{:T(128)}) while((s32[]{:T(128)}, bf16[3,512,128]{2,1,0:T(8,128)(2,1)}, bf16[3,512,1,128]{3,1,2,0:T(8,128)(2,1)S(1)}, ...), condition=%wide.region_9.10_spmd, body=%wide.region_6.9_spmd.sunk | while | flops 819526656 | bytes 23865456 | solution.py:31
  231.3 2.1 fusion.49
  235.6 2.1 fusion.49
  244.0 9.8 %all-to-all-start.7 = ((bf16[32,48,128]{2,1,0:T(8,128)(2,1)}), bf16[32,48,128]{2,1,0:T(8,128)(2,1)S(1)}, u32[]{:S(2)}, u32[]{:S(2)}) async-start(bf16[32,48,128]{2,1,0:T(8,128)(2,1)} %broadcast_select_fusion), calls=%async_computation.7 | async-start | bytes 786432 | tf_op jit(solution)/shard_map/all_to_all | solution.py:71
  253.8 31.2 %while.20 = (s32[]{:T(128)}, bf16[6,512,128]{2,1,0:T(8,128)(2,1)}, bf16[6,512,1,128]{3,1,2,0:T(8,128)(2,1)}, bf16[3072,1,128]{2,0,1:T(8,128)(2,1)S(1)}, bf16[3072,1,128]{2,0,1:T(8,128)(2,1)S(1)}, /*index=5*/s32[]{:T(128)}) while((s32[]{:T(128)}, bf16[6,512,128]{2,1,0:T(8,128)(2,1)}, bf16[6,512,1,128]{3,1,2,0:T(8,128)(2,1)}, ...), condition=%wide.region_3.4_spmd, body=%wide.region_0.3_spmd.sunk | while | flops 819526656 | bytes 20719700 | solution.py:31
  256.9 2.1 fusion.46
  262.1 2.1 fusion.46
  267.3 2.1 fusion.46
  272.5 2.1 fusion.46
  277.7 2.1 fusion.46
  282.9 2.1 fusion.46
  285.0 9.8 %all-to-all-start.3 = ((bf16[32,96,128]{2,1,0:T(8,128)(2,1)}), bf16[32,96,128]{2,1,0:T(8,128)(2,1)S(1)}, u32[]{:S(2)}, u32[]{:S(2)}) async-start(bf16[32,96,128]{2,1,0:T(8,128)(2,1)} %bitcast.145), calls=%async_computation.3 | async-start | bytes 1572864 | tf_op jit(solution)/shard_map/all_to_all | solution.py:70
  295.6 13.8 %all-to-all-done.3 = bf16[32,96,128]{2,1,0:T(8,128)(2,1)S(1)} async-done(((bf16[32,96,128]{2,1,0:T(8,128)(2,1)}), bf16[32,96,128]{2,1,0:T(8,128)(2,1)S(1)}, u32[]{:S(2)}, u32[]{:S(2)}) %all-to-all-start.3) | async-done | bytes 786464 | tf_op jit(solution)/shard_map/all_to_all | solution.py:70
  (61 shorter events, 38.8 us)
Async XLA Ops:
  0.6 1.1 copy-start
  0.6 41.3 %copy-start.3 = (bf16[96,4096]{1,0:T(8,128)(2,1)S(1)}, bf16[96,4096]{1,0:T(8,128)(2,1)}, u32[]{:S(2)}) copy-start(bf16[96,4096]{1,0:T(8,128)(2,1)} %param.15) | copy-start | bytes 2359300
  2.8 32.7 %all-to-all-start.1 = ((bf16[96,32,128]{2,0,1:T(8,128)(2,1)}), bf16[96,32,128]{2,0,1:T(8,128)(2,1)S(1)}, u32[]{:S(2)}, u32[]{:S(2)}) async-start(bf16[96,32,128]{2,0,1:T(8,128)(2,1)} %copy_bitcast_fusion.5), calls=%async_computation.1 | async-start | bytes 1572864 | tf_op jit(solution)/shard_map/all_to_all | solution.py:43
  13.9 109.2 %copy-start.7 = (u32[256]{0:T(256)S(1)}, u32[256]{0:T(256)}, u32[]{:S(2)}) copy-start(u32[256]{0:T(256)} %constant.52) | copy-start | bytes 3076
  13.9 132.9 %copy-start.6 = (s32[1,48]{1,0:T(1,128)S(1)}, s32[1,48]{1,0:T(1,128)}, u32[]{:S(2)}) copy-start(s32[1,48]{1,0:T(1,128)} %param.18) | copy-start | bytes 580
  35.5 26.8 %all-to-all-start.2 = ((bf16[96,32,128]{2,0,1:T(8,128)(2,1)}), bf16[96,32,128]{2,0,1:T(8,128)(2,1)S(1)}, u32[]{:S(2)}, u32[]{:S(2)}) async-start(bf16[96,32,128]{2,0,1:T(8,128)(2,1)} %copy_bitcast_fusion.4), calls=%async_computation.2 | async-start | bytes 1572864 | tf_op jit(solution)/shard_map/all_to_all | solution.py:44
  62.3 0.9 copy-start.1
  63.2 26.4 %all-to-all-start.4 = ((bf16[96,32,128]{2,0,1:T(8,128)(2,1)}), bf16[96,32,128]{2,0,1:T(8,128)(2,1)S(1)}, u32[]{:S(2)}, u32[]{:S(2)}) async-start(bf16[96,32,128]{2,0,1:T(8,128)(2,1)} %copy_bitcast_fusion.3), calls=%async_computation.4 | async-start | bytes 1572864 | tf_op jit(solution)/shard_map/all_to_all | solution.py:47
  69.7 114.5 %copy-start.4 = (bf16[96,4096]{1,0:T(8,128)(2,1)S(1)}, bf16[96,4096]{1,0:T(8,128)(2,1)}, u32[]{:S(2)}) copy-start(bf16[96,4096]{1,0:T(8,128)(2,1)} %param.12) | copy-start | bytes 2359300
  89.6 26.4 %all-to-all-start.5 = ((bf16[96,32,128]{2,0,1:T(8,128)(2,1)}), bf16[96,32,128]{2,0,1:T(8,128)(2,1)}, u32[]{:S(2)}, u32[]{:S(2)}) async-start(bf16[96,32,128]{2,0,1:T(8,128)(2,1)} %copy_bitcast_fusion.2), calls=%async_computation.5 | async-start | bytes 1572864 | tf_op jit(solution)/shard_map/all_to_all | solution.py:48
  116.0 88.9 %all-to-all-start.6 = ((bf16[96,32,128]{2,0,1:T(8,128)(2,1)}), bf16[96,32,128]{2,0,1:T(8,128)(2,1)}, u32[]{:S(2)}, u32[]{:S(2)}) async-start(bf16[96,32,128]{2,0,1:T(8,128)(2,1)} %copy_bitcast_fusion.1), calls=%async_computation.6 | async-start | bytes 1572864 | tf_op jit(solution)/shard_map/all_to_all | solution.py:49
  204.8 39.2 %all-to-all-start = ((bf16[96,32,128]{2,0,1:T(8,128)(2,1)}), bf16[96,32,128]{2,0,1:T(8,128)(2,1)}, u32[]{:S(2)}, u32[]{:S(2)}) async-start(bf16[96,32,128]{2,0,1:T(8,128)(2,1)} %copy_bitcast_fusion.6), calls=%async_computation | async-start | bytes 1572864 | tf_op jit(solution)/shard_map/all_to_all | solution.py:42
  229.1 24.7 %copy-start.2 = (bf16[96,32,128]{2,0,1:T(8,128)(2,1)S(1)}, bf16[96,32,128]{2,0,1:T(8,128)(2,1)}, u32[]{:S(2)}) copy-start(bf16[96,32,128]{2,0,1:T(8,128)(2,1)} %copy-done.1) | copy-start | bytes 2359300
  229.1 2.2 copy-start.5
  233.4 2.2 copy-start.5
  237.7 2.2 copy-start.5
  244.0 41.0 %all-to-all-start.7 = ((bf16[32,48,128]{2,1,0:T(8,128)(2,1)}), bf16[32,48,128]{2,1,0:T(8,128)(2,1)S(1)}, u32[]{:S(2)}, u32[]{:S(2)}) async-start(bf16[32,48,128]{2,1,0:T(8,128)(2,1)} %broadcast_select_fusion), calls=%async_computation.7 | async-start | bytes 786432 | tf_op jit(solution)/shard_map/all_to_all | solution.py:71
  285.0 24.4 %all-to-all-start.3 = ((bf16[32,96,128]{2,1,0:T(8,128)(2,1)}), bf16[32,96,128]{2,1,0:T(8,128)(2,1)S(1)}, u32[]{:S(2)}, u32[]{:S(2)}) async-start(bf16[32,96,128]{2,1,0:T(8,128)(2,1)} %bitcast.145), calls=%async_computation.3 | async-start | bytes 1572864 | tf_op jit(solution)/shard_map/all_to_all | solution.py:70
where the time goes:
time: 313 us; the launch traced here: 310 us
  waiting for transfers between devices  88 us (28%)
  starting transfers between devices  64.8 us (21%)
  blocking collectives  58.6 us (19%)
  local copies, waits for them, and re-layouts  50.6 us (16%)
  matrix products  33.5 us (11%)
  other arithmetic  13.3 us (4%)
    all_gather x1, blocking collectives, per_device(): lax.all_gather(masked_rows, 'seq', axis=0, tiled=True)  36.5 us
    unnamed x1, blocking collectives  22 us
    all_to_all x1, waiting for transfers between devices, per_device(): lax.all_to_all(keys, 'seq', split_axis=1, concat_axis=0, tiled=True)  19.4 us
    all_to_all x1, waiting for transfers between devices, per_device(): lax.all_to_all(values, 'seq', split_axis=1, concat_axis=0, tiled=True)  19.4 us
    dot_general x9, matrix products, one_block(): jnp.einsum('hqk,khd->qhd', weights, value_heads, preferred_element_type=j...  18.6 us
    all_to_all x1, waiting for transfers between devices, per_device(): lax.all_to_all(outgoing[1], 'seq', split_axis=1, concat_axis=0, tiled=True)  17.7 us
    all_to_all x1, waiting for transfers between devices, per_device(): lax.all_to_all(outgoing[0], 'seq', split_axis=1, concat_axis=0, tiled=True)  17.7 us
    scatter x1, local copies, waits for them, and re-layouts, per_device(): cache_values = head_values.at[target].set(new_values, mode='drop')  16 us
  transfers between devices with their start and end apart: 8, of which 5 were waited for; matrix products, arithmetic and copies ran while one was open for 30% of the time, Pallas kernels for 0%

commit v1 on v0

v1 whole, which is shorter than its diff:
```python
import functools
import math

import jax
import jax.numpy as jnp
from jax import lax
from jax.experimental import pallas as pl
from jax.experimental.pallas import tpu as pltpu
from jax.sharding import PartitionSpec as P

HEAD_DIM = 128
MESH = pl.DeviceIdType.MESH
KEY_CHUNK = 512
EXP2_SCALE = math.log2(math.e) / math.sqrt(HEAD_DIM)


def attend(query_block, key_ref, value_ref, score_ref):
    tokens = key_ref.shape[0]
    rows = query_block.shape[0]
    top = None
    for c in range(0, tokens, KEY_CHUNK):
        scores = lax.dot_general(
            query_block,
            key_ref[pl.ds(c, KEY_CHUNK), :],
            (((1,), (1,)), ((), ())),
            preferred_element_type=jnp.float32,
        )
        score_ref[:, pl.ds(c, KEY_CHUNK)] = scores
        for g in range(0, KEY_CHUNK, HEAD_DIM):
            part = scores[:, g : g + HEAD_DIM]
            top = part if top is None else jnp.maximum(top, part)
    top = jnp.max(top, axis=-1, keepdims=True)
    total = jnp.zeros((rows, 2 * HEAD_DIM), jnp.float32)
    for c in range(0, tokens, KEY_CHUNK):
        powers = jnp.exp2((score_ref[:, pl.ds(c, KEY_CHUNK)] - top) * EXP2_SCALE)
        total += jnp.dot(
            powers.astype(jnp.bfloat16),
            value_ref[pl.ds(c, KEY_CHUNK), :],
            preferred_element_type=jnp.float32,
        )
    return total[:, :HEAD_DIM] / total[:, HEAD_DIM:]


def kernel(
    shards,
    q_ref,
    k_ref,
    v_ref,
    fq_ref,
    fk_ref,
    fv_ref,
    rows_ref,
    count_ref,
    refresh_ref,
    cached_ref,
    q_buf,
    k_buf,
    v_buf,
    fresh_own,
    fresh_out,
    fresh_buf,
    list_out,
    list_buf,
    score_buf,
    refresh_buf,
    cached_buf,
    load_sem,
    send_sem,
    recv_sem,
):
    me = lax.axis_index("seq")
    own = q_ref.shape[0]
    slots = rows_ref.shape[1]

    def peer(i):
        return lax.rem(me + i, shards)

    def columns(head):
        return pl.ds(pl.multiple_of(head * HEAD_DIM, HEAD_DIM), HEAD_DIM)

    def rows_of(shard):
        return pl.ds(pl.multiple_of(shard * own, own), own)

    loads = [
        pltpu.make_async_copy(ref, fresh_own.at[i], load_sem.at[i])
        for i, ref in enumerate((fq_ref, fk_ref, fv_ref))
    ]
    for load in loads:
        load.start()

    barrier = pltpu.get_barrier_semaphore()

    def greet(i, carry):
        pl.semaphore_signal(barrier, inc=1, device_id={"seq": peer(i)}, device_id_type=MESH)
        return carry

    lax.fori_loop(1, shards, greet, 0)
    pl.semaphore_wait(barrier, shards - 1)

    stage_a = ((k_ref, k_buf, 0), (v_ref, v_buf, 1), (q_ref, q_buf, 2))

    def send_a(i, carry):
        to = peer(i)
        for ref, buf, n in stage_a:
            pltpu.make_async_remote_copy(
                src_ref=ref.at[:, columns(to)],
                dst_ref=buf.at[rows_of(me), pl.ds(0, HEAD_DIM)],
                send_sem=send_sem.at[n],
                recv_sem=recv_sem.at[n],
                device_id={"seq": to},
                device_id_type=MESH,
            ).start()
        return carry

    lax.fori_loop(1, shards, send_a, 0)
    for ref, buf, n in stage_a:
        pltpu.make_async_copy(
            ref.at[:, columns(me)], buf.at[rows_of(me), pl.ds(0, HEAD_DIM)], recv_sem.at[n]
        ).start()

    count = count_ref[0]
    listed = rows_ref[...]
    lane = lax.broadcasted_iota(jnp.int32, (1, slots), 1)
    list_out[...] = jnp.full(list_out.shape, count, jnp.int32)
    list_out[0:1, 0:slots] = jnp.where(lane < count, listed, -1)
    pick = (lax.broadcasted_iota(jnp.int32, (own, slots), 0) == listed).astype(jnp.float32)
    pick = jnp.transpose(pick).astype(jnp.bfloat16)
    for load in loads:
        load.wait()

    def gather(head, carry):
        for i in range(3):
            fresh_out[head, :, pl.ds(i * HEAD_DIM, HEAD_DIM)] = jnp.dot(
                pick, fresh_own[i, :, columns(head)], preferred_element_type=jnp.float32
            ).astype(jnp.bfloat16)
        return carry

    lax.fori_loop(0, shards, gather, 0)

    def send_b(i, carry):
        to = peer(i)
        for src, dst, n in (
            (fresh_out.at[to], fresh_buf.at[me], 3),
            (list_out, list_buf.at[me], 4),
        ):
            pltpu.make_async_remote_copy(
                src_ref=src,
                dst_ref=dst,
                send_sem=send_sem.at[n],
                recv_sem=recv_sem.at[n],
                device_id={"seq": to},
                device_id_type=MESH,
            ).start()
        return carry

    lax.fori_loop(1, shards, send_b, 0)
    pltpu.make_async_copy(fresh_out.at[me], fresh_buf.at[me], recv_sem.at[3]).start()
    pltpu.make_async_copy(list_out, list_buf.at[me], recv_sem.at[4]).start()

    v_buf[:, HEAD_DIM:] = jnp.ones((v_buf.shape[0], HEAD_DIM), jnp.bfloat16)

    def arrived(ref, n):
        pltpu.make_async_copy(ref, ref, recv_sem.at[n]).wait()

    arrived(k_buf, 0)
    arrived(v_buf.at[:, pl.ds(0, HEAD_DIM)], 1)
    arrived(q_buf, 2)

    def send_home(src, dst, to, n):
        @pl.when(to != me)
        def _():
            pltpu.make_async_remote_copy(
                src_ref=src,
                dst_ref=dst,
                send_sem=send_sem.at[n],
                recv_sem=recv_sem.at[n],
                device_id={"seq": to},
                device_id_type=MESH,
            ).start()

        @pl.when(to == me)
        def _():
            pltpu.make_async_copy(src, dst, recv_sem.at[n]).start()

    def refresh(i, carry):
        block = pl.ds(pl.multiple_of(i * 2 * own, 2 * own), 2 * own)
        out = attend(q_buf[block, :], k_buf, v_buf, score_buf)
        refresh_buf[block, :] = out.astype(jnp.bfloat16)
        for j in range(2):
            to = 2 * i + j
            send_home(refresh_buf.at[rows_of(to)], refresh_ref.at[:, columns(me)], to, 5)
        return carry

    lax.fori_loop(0, shards // 2, refresh, 0)

    arrived(fresh_buf, 3)
    arrived(list_buf, 4)

    def update(shard, carry):
        at = list_buf[shard, 0:1, 0:slots]
        put = lax.broadcasted_iota(jnp.int32, (own, slots), 0) == at
        put = put.astype(jnp.float32)
        changed = jnp.max(put, axis=-1, keepdims=True) > 0.0
        new = jnp.dot(
            put.astype(jnp.bfloat16),
            fresh_buf[shard, :, HEAD_DIM:],
            preferred_element_type=jnp.float32,
        ).astype(jnp.bfloat16)
        block = rows_of(shard)
        k_buf[block, :] = jnp.where(changed, new[:, :HEAD_DIM], k_buf[block, :])
        v_buf[block, :HEAD_DIM] = jnp.where(
            changed, new[:, HEAD_DIM:], v_buf[block, :HEAD_DIM]
        )
        return carry

    lax.fori_loop(0, shards, update, 0)

    def cached(i, carry):
        group = pl.ds(4 * i, 4)
        query_block = fresh_buf[group, :, 0:HEAD_DIM].reshape(4 * slots, HEAD_DIM)
        out = attend(query_block, k_buf, v_buf, score_buf)
        out = out.reshape(4, slots, HEAD_DIM)
        slot = lax.broadcasted_iota(jnp.int32, out.shape, 1)
        live = slot < list_buf[group, 1:2, :]
        cached_buf[group, :, :] = jnp.where(live, out, 0.0).astype(jnp.bfloat16)
        for j in range(4):
            to = 4 * i + j
            send_home(cached_buf.at[to], cached_ref.at[:, columns(me)], to, 6)
        return carry

    lax.fori_loop(0, shards // 4, cached, 0)

    arrived(refresh_ref, 5)
    arrived(cached_ref, 6)

    def sent(ref, n):
        pltpu.make_async_copy(ref, ref, send_sem.at[n]).wait()

    others = pl.ds(0, (shards - 1) * own)
    for n in (0, 1, 2, 5):
        sent(q_buf.at[others, :], n)
    sent(fresh_buf.at[pl.ds(0, shards - 1)], 3)
    sent(list_buf.at[pl.ds(0, shards - 1)], 4)
    sent(cached_buf.at[pl.ds(0, shards - 1)], 6)


def per_device(
    queries, keys, values, fresh_queries, fresh_keys, fresh_values, masked_rows, masked_counts
):
    own, width = queries.shape
    slots = masked_rows.shape[1]
    shards = lax.axis_size("seq")
    tokens = shards * own
    bf16 = jnp.bfloat16
    hbm = pl.BlockSpec(memory_space=pl.ANY)
    return pl.pallas_call(
        functools.partial(kernel, shards),
        name="attention",
        out_shape=(
            jax.ShapeDtypeStruct((own, width), bf16),
            jax.ShapeDtypeStruct((slots, width), bf16),
        ),
        in_specs=[hbm] * 6
        + [pl.BlockSpec(memory_space=pltpu.VMEM), pl.BlockSpec(memory_space=pltpu.SMEM)],
        out_specs=(hbm, hbm),
        scratch_shapes=[
            pltpu.VMEM((tokens, HEAD_DIM), bf16),
            pltpu.VMEM((tokens, HEAD_DIM), bf16),
            pltpu.VMEM((tokens, 2 * HEAD_DIM), bf16),
            pltpu.VMEM((3, own, width), bf16),
            pltpu.VMEM((shards, slots, 3 * HEAD_DIM), bf16),
            pltpu.VMEM((shards, slots, 3 * HEAD_DIM), bf16),
            pltpu.VMEM((2, HEAD_DIM), jnp.int32),
            pltpu.VMEM((shards, 2, HEAD_DIM), jnp.int32),
            pltpu.VMEM((2 * own, tokens), jnp.float32),
            pltpu.VMEM((tokens, HEAD_DIM), bf16),
            pltpu.VMEM((shards, slots, HEAD_DIM), bf16),
            pltpu.SemaphoreType.DMA((3,)),
            pltpu.SemaphoreType.DMA((7,)),
            pltpu.SemaphoreType.DMA((7,)),
        ],
        compiler_params=pltpu.CompilerParams(
            collective_id=0, has_side_effects=True, vmem_limit_bytes=40 * 2**20
        ),
        cost_estimate=pl.CostEstimate(
            flops=6 * tokens * tokens * HEAD_DIM,
            bytes_accessed=12 * own * width,
            transcendentals=tokens * tokens * 3 // 2,
        ),
    )(
        queries,
        keys,
        values,
        fresh_queries,
        fresh_keys,
        fresh_values,
        masked_rows,
        masked_counts,
    )


def solution(mesh):
    spread = P(("doc", "seq"), None)
    return jax.shard_map(
        per_device,
        mesh=mesh,
        in_specs=(spread,) * 7 + (P(("doc", "seq")),),
        out_specs=(spread, spread),
        check_vma=False,
    )
```

time: 313 us -> 127 us (0.41)
  Pallas kernels: 0 us -> 115 us
  waiting for transfers between devices: 88 us -> 0 us
  starting transfers between devices: 64.8 us -> 0 us
  blocking collectives: 58.6 us -> 0 us
  local copies, waits for them, and re-layouts: 50.6 us -> 8.42 us
  matrix products: 33.5 us -> 0 us
  other arithmetic: 13.3 us -> 0 us
    pallas_call x0 -> x1, Pallas kernels: none -> 115 us  [per_device(): pl.pallas_call(functools.partial(kernel, shards), name='attention', out_s...]
    all_to_all x8 -> x0, waiting for transfers between devices: 88 us -> none  [the longest x1 19.4 us: per_device(): lax.all_to_all(keys, 'seq', split_axis=1, concat_axis=0, tiled=True)]
    all_to_all x8 -> x0, starting transfers between devices: 64.8 us -> none  [the longest x1 11.1 us: per_device(): lax.all_to_all(keys, 'seq', split_axis=1, concat_axis=0, tiled=True)]
    all_gather x1 -> x0, blocking collectives: 36.5 us -> none  [per_device(): lax.all_gather(masked_rows, 'seq', axis=0, tiled=True)]
    dot_general x18 -> x0, matrix products: 33.5 us -> none  [the longest x9 18.6 us: one_block(): jnp.einsum('hqk,khd->qhd', weights, value_heads, preferred_element_type=j...]
    scatter x2 -> x0, local copies, waits for them, and re-layouts: 30.2 us -> none  [the longest x1 16 us: per_device(): cache_values = head_values.at[target].set(new_values, mode='drop')]
    unnamed x1 -> x0, blocking collectives: 22 us -> none
    all_to_all x8 -> x0, local copies, waits for them, and re-layouts: 11.3 us -> none  [the longest x1 2.24 us: per_device(): lax.all_to_all(outgoing[1], 'seq', split_axis=1, concat_axis=0, tiled=True)]
  transfers between devices with their start and end apart: 8 -> 0, of which waited for: 5 -> 0; matrix products, arithmetic and copies ran while one was open for 30% -> 0% of each run, Pallas kernels for 0% -> 0%
where the time goes in v1:
time: 127 us; the launch traced here: 125 us
  Pallas kernels  115 us (91%)
  local copies, waits for them, and re-layouts  8.42 us (7%)
  between operations  1.33 us (1%)
    pallas_call x1, Pallas kernels, per_device(): pl.pallas_call(functools.partial(kernel, shards), name='attention', out_s...  115 us
    unnamed x16, local copies, waits for them, and re-layouts  8.42 us

profile of v1, /device:TPU:62, one launch (start us, length us, event | category | flops | bytes accessed | tf_op | source)
XLA Modules:
  0.0 124.9 jit_solution(9469803238082769406)
XLA Ops:
  0.6 0.0 copy-start.6
  1.3 0.0 copy-done.6
  1.3 0.0 copy-start
  1.3 1.1 copy-done
  2.4 0.0 copy-start.1
  2.4 1.1 copy-done.1
  3.6 0.0 copy-start.2
  3.6 1.1 copy-done.2
  4.7 0.0 copy-start.3
  4.7 1.1 copy-done.3
  5.8 0.0 copy-start.4
  5.8 1.1 copy-done.4
  7.0 0.0 copy-start.5
  7.0 1.1 copy-done.5
  8.1 115.2 %attention.1 = (bf16[96,4096]{1,0:T(8,128)(2,1)S(1)}, bf16[48,4096]{1,0:T(8,128)(2,1)S(1)}) custom-call(bf16[96,4096]{1,0:T(8,128)(2,1)S(1)} %copy-done, bf16[96,4096]{1,0:T(8,128)(2,1)S(1)} %copy-done.1, bf16[96,4096]{1,0:T(8,128)(2,1)S(1)} %copy-done.2, bf16[96,4096]{1,0:T(8,128)(2,1)S(1)} %copy-done.3, bf16[96,4096]{1,0:T(8,128)(2,1)S(1)} %copy-done.4, ...), custom_call_target="tpu_custom_call" | custom-call | flops 7247757312 | bytes 4718592 | tf_op jit(solution)/shard_map/attention/pallas_call | solution.py:256
  123.3 0.9 copy.13
  124.2 0.7 copy.14
Async XLA Ops:
  0.6 0.7 copy-start.6
  1.3 1.1 copy-start
  2.4 1.1 copy-start.1
  3.6 1.1 copy-start.2
  4.7 1.1 copy-start.3
  5.8 1.1 copy-start.4
  7.0 1.1 copy-start.5

commit v2 on v1

--- a/solution.py
+++ b/solution.py
@@ -9,35 +9,30 @@
 from jax.sharding import PartitionSpec as P
 
 HEAD_DIM = 128
+PLANES = 8
+VMEM_LIMIT = 105 * 2**19
 MESH = pl.DeviceIdType.MESH
-KEY_CHUNK = 512
+KEY_CHUNK = 256
 EXP2_SCALE = math.log2(math.e) / math.sqrt(HEAD_DIM)
 
 
-def attend(query_block, key_ref, value_ref, score_ref):
-    tokens = key_ref.shape[0]
+def attend(query_block, key_ref, value_ref):
     rows = query_block.shape[0]
-    top = None
-    for c in range(0, tokens, KEY_CHUNK):
+    top = jnp.full((rows, 1), -jnp.inf, jnp.float32)
+    total = jnp.zeros((rows, 2 * HEAD_DIM), jnp.float32)
+    for c in range(0, key_ref.shape[0], KEY_CHUNK):
         scores = lax.dot_general(
             query_block,
             key_ref[pl.ds(c, KEY_CHUNK), :],
             (((1,), (1,)), ((), ())),
             preferred_element_type=jnp.float32,
         )
-        score_ref[:, pl.ds(c, KEY_CHUNK)] = scores
-        for g in range(0, KEY_CHUNK, HEAD_DIM):
-            part = scores[:, g : g + HEAD_DIM]
-            top = part if top is None else jnp.maximum(top, part)
-    top = jnp.max(top, axis=-1, keepdims=True)
-    total = jnp.zeros((rows, 2 * HEAD_DIM), jnp.float32)
-    for c in range(0, tokens, KEY_CHUNK):
-        powers = jnp.exp2((score_ref[:, pl.ds(c, KEY_CHUNK)] - top) * EXP2_SCALE)
-        total += jnp.dot(
-            powers.astype(jnp.bfloat16),
-            value_ref[pl.ds(c, KEY_CHUNK), :],
-            preferred_element_type=jnp.float32,
+        new_top = jnp.maximum(top, jnp.max(scores, axis=-1, keepdims=True))
+        powers = jnp.exp2((scores - new_top) * EXP2_SCALE).astype(jnp.bfloat16)
+        total = total * jnp.exp2((top - new_top) * EXP2_SCALE) + jnp.dot(
+            powers, value_ref[pl.ds(c, KEY_CHUNK), :], preferred_element_type=jnp.float32
         )
+        top = new_top
     return total[:, :HEAD_DIM] / total[:, HEAD_DIM:]
 
 
@@ -61,7 +56,6 @@
     fresh_buf,
     list_out,
     list_buf,
-    score_buf,
     refresh_buf,
     cached_buf,
     load_sem,
@@ -69,11 +63,20 @@
     recv_sem,
 ):
     me = lax.axis_index("seq")
+    width = shards // PLANES
     own = q_ref.shape[0]
     slots = rows_ref.shape[1]
 
+    def plane(i):
+        step = PLANES // 2 + lax.div(i + 1, 2) * (1 - 2 * lax.rem(i, 2))
+        return lax.rem(lax.div(me, width) + step, PLANES)
+
     def peer(i):
-        return lax.rem(me + i, shards)
+        reach = PLANES - 1
+        far = lax.div(i, reach) < width
+        step = jnp.where(far, lax.div(i, reach) + 1, i - reach * width + 1)
+        x = lax.rem(lax.rem(me, width) + step, width)
+        return plane(jnp.where(far, lax.rem(i, reach), reach)) * width + x
 
     def columns(head):
         return pl.ds(pl.multiple_of(head * HEAD_DIM, HEAD_DIM), HEAD_DIM)
@@ -94,14 +97,15 @@
         pl.semaphore_signal(barrier, inc=1, device_id={"seq": peer(i)}, device_id_type=MESH)
         return carry
 
-    lax.fori_loop(1, shards, greet, 0)
+    lax.fori_loop(0, shards - 1, greet, 0)
     pl.semaphore_wait(barrier, shards - 1)
 
     stage_a = ((k_ref, k_buf, 0), (v_ref, v_buf, 1), (q_ref, q_buf, 2))
 
-    def send_a(i, carry):
-        to = peer(i)
-        for ref, buf, n in stage_a:
+    for ref, buf, n in stage_a:
+
+        def send_a(i, carry):
+            to = peer(i)
             pltpu.make_async_remote_copy(
                 src_ref=ref.at[:, columns(to)],
                 dst_ref=buf.at[rows_of(me), pl.ds(0, HEAD_DIM)],
@@ -110,17 +114,19 @@
                 device_id={"seq": to},
                 device_id_type=MESH,
             ).start()
-        return carry
-
-    lax.fori_loop(1, shards, send_a, 0)
+            return carry
+
+        lax.fori_loop(0, shards - 1, send_a, 0)
     for ref, buf, n in stage_a:
         pltpu.make_async_copy(
             ref.at[:, columns(me)], buf.at[rows_of(me), pl.ds(0, HEAD_DIM)], recv_sem.at[n]
         ).start()
 
     count = count_ref[0]
-    listed = rows_ref[...]
     lane = lax.broadcasted_iota(jnp.int32, (1, slots), 1)
+    listed = jnp.zeros((1, slots), jnp.int32)
+    for j in range(slots):
+        listed = jnp.where(lane == j, rows_ref[0, j], listed)
     list_out[...] = jnp.full(list_out.shape, count, jnp.int32)
     list_out[0:1, 0:slots] = jnp.where(lane < count, listed, -1)
     pick = (lax.broadcasted_iota(jnp.int32, (own, slots), 0) == listed).astype(jnp.float32)
@@ -153,7 +159,7 @@
             ).start()
         return carry
 
-    lax.fori_loop(1, shards, send_b, 0)
+    lax.fori_loop(0, shards - 1, send_b, 0)
     pltpu.make_async_copy(fresh_out.at[me], fresh_buf.at[me], recv_sem.at[3]).start()
     pltpu.make_async_copy(list_out, list_buf.at[me], recv_sem.at[4]).start()
 
@@ -183,52 +189,58 @@
             pltpu.make_async_copy(src, dst, recv_sem.at[n]).start()
 
     def refresh(i, carry):
-        block = pl.ds(pl.multiple_of(i * 2 * own, 2 * own), 2 * own)
-        out = attend(q_buf[block, :], k_buf, v_buf, score_buf)
+        first = plane(i) * width
+        block = pl.ds(pl.multiple_of(first * own, width * own), width * own)
+        out = attend(q_buf[block, :], k_buf, v_buf)
         refresh_buf[block, :] = out.astype(jnp.bfloat16)
-        for j in range(2):
-            to = 2 * i + j
+        for j in range(width):
+            to = first + j
             send_home(refresh_buf.at[rows_of(to)], refresh_ref.at[:, columns(me)], to, 5)
         return carry
 
-    lax.fori_loop(0, shards // 2, refresh, 0)
+    lax.fori_loop(0, PLANES, refresh, 0)
 
     arrived(fresh_buf, 3)
     arrived(list_buf, 4)
 
-    def update(shard, carry):
-        at = list_buf[shard, 0:1, 0:slots]
-        put = lax.broadcasted_iota(jnp.int32, (own, slots), 0) == at
-        put = put.astype(jnp.float32)
-        changed = jnp.max(put, axis=-1, keepdims=True) > 0.0
-        new = jnp.dot(
-            put.astype(jnp.bfloat16),
-            fresh_buf[shard, :, HEAD_DIM:],
-            preferred_element_type=jnp.float32,
-        ).astype(jnp.bfloat16)
-        block = rows_of(shard)
-        k_buf[block, :] = jnp.where(changed, new[:, :HEAD_DIM], k_buf[block, :])
-        v_buf[block, :HEAD_DIM] = jnp.where(
-            changed, new[:, HEAD_DIM:], v_buf[block, :HEAD_DIM]
-        )
-        return carry
-
-    lax.fori_loop(0, shards, update, 0)
+    def update(i, carry):
+        for j in range(width):
+            shard = i * width + j
+            at = list_buf[shard, 0:1, 0:slots]
+            put = lax.broadcasted_iota(jnp.int32, (own, slots), 0) == at
+            put = put.astype(jnp.float32)
+            changed = jnp.max(put, axis=-1, keepdims=True) > 0.0
+            new = jnp.dot(
+                put.astype(jnp.bfloat16),
+                fresh_buf[shard, :, HEAD_DIM:],
+                preferred_element_type=jnp.float32,
+            ).astype(jnp.bfloat16)
+            block = rows_of(shard)
+            k_buf[block, :] = jnp.where(changed, new[:, :HEAD_DIM], k_buf[block, :])
+            v_buf[block, :HEAD_DIM] = jnp.where(
+                changed, new[:, HEAD_DIM:], v_buf[block, :HEAD_DIM]
+            )
+        return carry
+
+    lax.fori_loop(0, PLANES, update, 0)
 
     def cached(i, carry):
-        group = pl.ds(4 * i, 4)
-        query_block = fresh_buf[group, :, 0:HEAD_DIM].reshape(4 * slots, HEAD_DIM)
-        out = attend(query_block, k_buf, v_buf, score_buf)
-        out = out.reshape(4, slots, HEAD_DIM)
-        slot = lax.broadcasted_iota(jnp.int32, out.shape, 1)
-        live = slot < list_buf[group, 1:2, :]
-        cached_buf[group, :, :] = jnp.where(live, out, 0.0).astype(jnp.bfloat16)
-        for j in range(4):
-            to = 4 * i + j
-            send_home(cached_buf.at[to], cached_ref.at[:, columns(me)], to, 6)
-        return carry
-
-    lax.fori_loop(0, shards // 4, cached, 0)
+        firsts = [plane(2 * i + j) * width for j in range(2)]
+        groups = [pl.ds(first, width) for first in firsts]
+        query_block = jnp.concatenate([fresh_buf[g, :, 0:HEAD_DIM] for g in groups])
+        out = attend(query_block.reshape(-1, HEAD_DIM), k_buf, v_buf)
+        out = out.reshape(2, width, slots, HEAD_DIM)
+        slot = lax.broadcasted_iota(jnp.int32, out.shape[1:], 1)
+        for j, group in enumerate(groups):
+            live = slot < list_buf[group, 1:2, :]
+            cached_buf[group, :, :] = jnp.where(live, out[j], 0.0).astype(jnp.bfloat16)
+        for first in firsts:
+            for j in range(width):
+                to = first + j
+                send_home(cached_buf.at[to], cached_ref.at[:, columns(me)], to, 6)
+        return carry
+
+    lax.fori_loop(0, PLANES // 2, cached, 0)
 
     arrived(refresh_ref, 5)
     arrived(cached_ref, 6)
@@ -252,7 +264,8 @@
     shards = lax.axis_size("seq")
     tokens = shards * own
     bf16 = jnp.bfloat16
-    hbm = pl.BlockSpec(memory_space=pl.ANY)
+    hbm = pl.BlockSpec(memory_space=pltpu.HBM)
+    anywhere = pl.BlockSpec(memory_space=pl.ANY)
     return pl.pallas_call(
         functools.partial(kernel, shards),
         name="attention",
@@ -260,9 +273,8 @@
             jax.ShapeDtypeStruct((own, width), bf16),
             jax.ShapeDtypeStruct((slots, width), bf16),
         ),
-        in_specs=[hbm] * 6
-        + [pl.BlockSpec(memory_space=pltpu.VMEM), pl.BlockSpec(memory_space=pltpu.SMEM)],
-        out_specs=(hbm, hbm),
+        in_specs=[hbm] * 6 + [pl.BlockSpec(memory_space=pltpu.SMEM)] * 2,
+        out_specs=(anywhere, anywhere),
         scratch_shapes=[
             pltpu.VMEM((tokens, HEAD_DIM), bf16),
             pltpu.VMEM((tokens, HEAD_DIM), bf16),
@@ -272,7 +284,6 @@
             pltpu.VMEM((shards, slots, 3 * HEAD_DIM), bf16),
             pltpu.VMEM((2, HEAD_DIM), jnp.int32),
             pltpu.VMEM((shards, 2, HEAD_DIM), jnp.int32),
-            pltpu.VMEM((2 * own, tokens), jnp.float32),
             pltpu.VMEM((tokens, HEAD_DIM), bf16),
             pltpu.VMEM((shards, slots, HEAD_DIM), bf16),
             pltpu.SemaphoreType.DMA((3,)),
@@ -280,7 +291,7 @@
             pltpu.SemaphoreType.DMA((7,)),
         ],
         compiler_params=pltpu.CompilerParams(
-            collective_id=0, has_side_effects=True, vmem_limit_bytes=40 * 2**20
+            collective_id=0, has_side_effects=True, vmem_limit_bytes=VMEM_LIMIT
         ),
         cost_estimate=pl.CostEstimate(
             flops=6 * tokens * tokens * HEAD_DIM,

time: 127 us -> 118 us (0.929)
  local copies, waits for them, and re-layouts: 8.42 us -> 1.63 us
    unnamed x16 -> x4, local copies, waits for them, and re-layouts: 8.42 us -> 1.63 us
    pallas_call x1, Pallas kernels: 115 us -> 114 us  [per_device(): pl.pallas_call(functools.partial(kernel, shards), name='attention', out_s...]
where the time goes in v2:
time: 118 us; the launch traced here: 117 us
  Pallas kernels  114 us (97%)
  local copies, waits for them, and re-layouts  1.63 us (1%)
  between operations  1.32 us (1%)
    pallas_call x1, Pallas kernels, per_device(): pl.pallas_call(functools.partial(kernel, shards), name='attention', out_s...  114 us

profile of v2, /device:TPU:62, one launch (start us, length us, event | category | flops | bytes accessed | tf_op | source)
XLA Modules:
  0.0 116.6 jit_solution(9300546150212657574)
XLA Ops:
  0.6 0.0 copy-start
  1.3 0.0 copy-done
  1.3 113.6 %attention.1 = (bf16[96,4096]{1,0:T(8,128)(2,1)S(1)}, bf16[48,4096]{1,0:T(8,128)(2,1)S(1)}) custom-call(bf16[96,4096]{1,0:T(8,128)(2,1)} %q_ref.1, bf16[96,4096]{1,0:T(8,128)(2,1)} %k_ref.1, bf16[96,4096]{1,0:T(8,128)(2,1)} %v_ref.1, bf16[96,4096]{1,0:T(8,128)(2,1)} %fq_ref.1, bf16[96,4096]{1,0:T(8,128)(2,1)} %fk_ref.1, bf16[96,4096]{1,0:T(8,128)(2,1)} %fv_ref.1, ...), custom_call_target="tpu_custom_call" | custom-call | flops 7247757312 | bytes 4718592 | tf_op jit(solution)/shard_map/attention/pallas_call | solution.py:269
  115.0 0.9 copy.13
  115.8 0.7 copy.14
Async XLA Ops:
  0.6 0.7 copy-start

commit v3 on v2

--- a/solution.py
+++ b/solution.py
@@ -78,12 +78,25 @@
         x = lax.rem(lax.rem(me, width) + step, width)
         return plane(jnp.where(far, lax.rem(i, reach), reach)) * width + x
 
+    def early_plane(i):
+        half = PLANES // 2
+        turn = lax.rem(i, half)
+        step = half // 2 + lax.div(turn + 1, 2) * (1 - 2 * lax.rem(turn, 2))
+        return lax.div(i, half) * half + lax.rem(lax.rem(lax.div(me, width), half) + step, half)
+
     def columns(head):
         return pl.ds(pl.multiple_of(head * HEAD_DIM, HEAD_DIM), HEAD_DIM)
 
     def rows_of(shard):
         return pl.ds(pl.multiple_of(shard * own, own), own)
 
+    barrier = pltpu.get_barrier_semaphore()
+
+    def greet(i, carry):
+        pl.semaphore_signal(barrier, inc=1, device_id={"seq": peer(i)}, device_id_type=MESH)
+        return carry
+
+    lax.fori_loop(0, shards - 1, greet, 0)
     loads = [
         pltpu.make_async_copy(ref, fresh_own.at[i], load_sem.at[i])
         for i, ref in enumerate((fq_ref, fk_ref, fv_ref))
@@ -91,13 +104,6 @@
     for load in loads:
         load.start()
 
-    barrier = pltpu.get_barrier_semaphore()
-
-    def greet(i, carry):
-        pl.semaphore_signal(barrier, inc=1, device_id={"seq": peer(i)}, device_id_type=MESH)
-        return carry
-
-    lax.fori_loop(0, shards - 1, greet, 0)
     pl.semaphore_wait(barrier, shards - 1)
 
     stage_a = ((k_ref, k_buf, 0), (v_ref, v_buf, 1), (q_ref, q_buf, 2))
@@ -225,14 +231,14 @@
     lax.fori_loop(0, PLANES, update, 0)
 
     def cached(i, carry):
-        firsts = [plane(2 * i + j) * width for j in range(2)]
+        firsts = [early_plane(2 * i + j) * width for j in range(2)]
         groups = [pl.ds(first, width) for first in firsts]
         query_block = jnp.concatenate([fresh_buf[g, :, 0:HEAD_DIM] for g in groups])
         out = attend(query_block.reshape(-1, HEAD_DIM), k_buf, v_buf)
         out = out.reshape(2, width, slots, HEAD_DIM)
         slot = lax.broadcasted_iota(jnp.int32, out.shape[1:], 1)
         for j, group in enumerate(groups):
-            live = slot < list_buf[group, 1:2, :]
+            live = slot < list_buf[group, 0:1, HEAD_DIM - 1 :]
             cached_buf[group, :, :] = jnp.where(live, out[j], 0.0).astype(jnp.bfloat16)
         for first in firsts:
             for j in range(width):
@@ -254,6 +260,17 @@
     sent(fresh_buf.at[pl.ds(0, shards - 1)], 3)
     sent(list_buf.at[pl.ds(0, shards - 1)], 4)
     sent(cached_buf.at[pl.ds(0, shards - 1)], 6)
+
+
+def hand_over(refresh_in, cached_in, refresh_ref, cached_ref, sem):
+    copies = [
+        pltpu.make_async_copy(refresh_in, refresh_ref, sem.at[0]),
+        pltpu.make_async_copy(cached_in, cached_ref, sem.at[1]),
+    ]
+    for copy in copies:
+        copy.start()
+    for copy in copies:
+        copy.wait()
 
 
 def per_device(
@@ -266,7 +283,7 @@
     bf16 = jnp.bfloat16
     hbm = pl.BlockSpec(memory_space=pltpu.HBM)
     anywhere = pl.BlockSpec(memory_space=pl.ANY)
-    return pl.pallas_call(
+    results = pl.pallas_call(
         functools.partial(kernel, shards),
         name="attention",
         out_shape=(
@@ -282,8 +299,8 @@
             pltpu.VMEM((3, own, width), bf16),
             pltpu.VMEM((shards, slots, 3 * HEAD_DIM), bf16),
             pltpu.VMEM((shards, slots, 3 * HEAD_DIM), bf16),
-            pltpu.VMEM((2, HEAD_DIM), jnp.int32),
-            pltpu.VMEM((shards, 2, HEAD_DIM), jnp.int32),
+            pltpu.VMEM((1, HEAD_DIM), jnp.int32),
+            pltpu.VMEM((shards, 1, HEAD_DIM), jnp.int32),
             pltpu.VMEM((tokens, HEAD_DIM), bf16),
             pltpu.VMEM((shards, slots, HEAD_DIM), bf16),
             pltpu.SemaphoreType.DMA((3,)),
@@ -308,6 +325,15 @@
         masked_rows,
         masked_counts,
     )
+    return pl.pallas_call(
+        hand_over,
+        name="hand_over",
+        out_shape=tuple(jax.ShapeDtypeStruct(r.shape, r.dtype) for r in results),
+        in_specs=[anywhere] * 2,
+        out_specs=(hbm, hbm),
+        scratch_shapes=[pltpu.SemaphoreType.DMA((2,))],
+        compiler_params=pltpu.CompilerParams(vmem_limit_bytes=2**20),
+    )(*results)
 
 
 def solution(mesh):

time: 118 us -> 115 us (0.975); the launches traced: 117 us -> 115 us
  local copies, waits for them, and re-layouts: 1.63 us -> 0.01 us
    unnamed x4 -> x2, local copies, waits for them, and re-layouts: 1.63 us -> 0.01 us
where the time goes in v3:
time: 115 us
  Pallas kernels  114 us (99%)
  between operations  1.31 us (1%)
    pallas_call x1, Pallas kernels, per_device(): pl.pallas_call(functools.partial(kernel, shards), name='attention', out_s...  113 us

profile of v3, /device:TPU:62, one launch (start us, length us, event | category | flops | bytes accessed | tf_op | source)
XLA Modules:
  0.0 115.4 jit_solution(15719340600926525192)
XLA Ops:
  0.6 0.0 copy-start
  1.3 0.0 copy-done
  1.3 113.0 %attention.1 = (bf16[96,4096]{1,0:T(8,128)(2,1)S(1)}, bf16[48,4096]{1,0:T(8,128)(2,1)S(1)}) custom-call(bf16[96,4096]{1,0:T(8,128)(2,1)} %q_ref.1, bf16[96,4096]{1,0:T(8,128)(2,1)} %k_ref.1, bf16[96,4096]{1,0:T(8,128)(2,1)} %v_ref.1, bf16[96,4096]{1,0:T(8,128)(2,1)} %fq_ref.1, bf16[96,4096]{1,0:T(8,128)(2,1)} %fk_ref.1, bf16[96,4096]{1,0:T(8,128)(2,1)} %fv_ref.1, ...), custom_call_target="tpu_custom_call" | custom-call | flops 7247757312 | bytes 4718592 | tf_op jit(solution)/shard_map/attention/pallas_call | solution.py:286
  114.4 1.0 hand_over.1
Async XLA Ops:
  0.6 0.7 copy-start

commit v4 on v3

--- a/solution.py
+++ b/solution.py
@@ -59,6 +59,7 @@
     refresh_buf,
     cached_buf,
     load_sem,
+    ready_sem,
     send_sem,
     recv_sem,
 ):
@@ -90,13 +91,21 @@
     def rows_of(shard):
         return pl.ds(pl.multiple_of(shard * own, own), own)
 
+    def device(dz, dx):
+        z = lax.rem(lax.div(me, width) + dz, PLANES)
+        return z * width + lax.rem(lax.rem(me, width) + dx, width)
+
+    def signal(sem, dz, dx):
+        pl.semaphore_signal(
+            sem, inc=1, device_id={"seq": device(dz, dx)}, device_id_type=MESH
+        )
+
+    plane_mates = [(0, dx) for dx in range(1, width)]
+    column_far, column_near = [(2, 0), (PLANES - 2, 0)], [(1, 0), (PLANES - 1, 0)]
     barrier = pltpu.get_barrier_semaphore()
-
-    def greet(i, carry):
-        pl.semaphore_signal(barrier, inc=1, device_id={"seq": peer(i)}, device_id_type=MESH)
-        return carry
-
-    lax.fori_loop(0, shards - 1, greet, 0)
+    for place in column_far + column_near + plane_mates:
+        signal(barrier, *place)
+
     loads = [
         pltpu.make_async_copy(ref, fresh_own.at[i], load_sem.at[i])
         for i, ref in enumerate((fq_ref, fk_ref, fv_ref))
@@ -104,25 +113,47 @@
     for load in loads:
         load.start()
 
-    pl.semaphore_wait(barrier, shards - 1)
-
     stage_a = ((k_ref, k_buf, 0), (v_ref, v_buf, 1), (q_ref, q_buf, 2))
 
-    for ref, buf, n in stage_a:
-
-        def send_a(i, carry):
-            to = peer(i)
-            pltpu.make_async_remote_copy(
-                src_ref=ref.at[:, columns(to)],
-                dst_ref=buf.at[rows_of(me), pl.ds(0, HEAD_DIM)],
-                send_sem=send_sem.at[n],
-                recv_sem=recv_sem.at[n],
-                device_id={"seq": to},
-                device_id_type=MESH,
-            ).start()
+    def send_a(n, places, columns_on):
+        ref, buf, _ = stage_a[n]
+
+        def one(c, carry):
+            for dz, dx in places:
+                to = device(dz, dx + c)
+                pltpu.make_async_remote_copy(
+                    src_ref=ref.at[:, columns(to)],
+                    dst_ref=buf.at[rows_of(me), pl.ds(0, HEAD_DIM)],
+                    send_sem=send_sem.at[n],
+                    recv_sem=recv_sem.at[n],
+                    device_id={"seq": to},
+                    device_id_type=MESH,
+                ).start()
             return carry
 
-        lax.fori_loop(0, shards - 1, send_a, 0)
+        lax.fori_loop(*columns_on, one, 0)
+
+    own_column, other_columns, all_columns = (0, 1), (1, width), (0, width)
+    near = column_far + column_near
+    far = [(PLANES // 2, 0), (PLANES // 2 - 1, 0), (PLANES // 2 + 1, 0)]
+
+    pl.semaphore_wait(barrier, len(near) + len(plane_mates))
+    for place in column_far + plane_mates:
+        signal(ready_sem.at[0], *place)
+    send_a(0, near, own_column)
+    send_a(1, near, own_column)
+    pl.semaphore_wait(ready_sem.at[0], len(column_far) + len(plane_mates))
+    for place in plane_mates:
+        signal(ready_sem.at[1], *place)
+    send_a(0, far, own_column)
+    send_a(0, near, other_columns)
+    pl.semaphore_wait(ready_sem.at[1], len(plane_mates))
+    send_a(0, far, other_columns)
+    send_a(1, far, own_column)
+    send_a(1, far + near, other_columns)
+    send_a(2, far + near, all_columns)
+    for n in range(3):
+        send_a(n, [(0, 0)], other_columns)
     for ref, buf, n in stage_a:
         pltpu.make_async_copy(
             ref.at[:, columns(me)], buf.at[rows_of(me), pl.ds(0, HEAD_DIM)], recv_sem.at[n]
@@ -304,6 +335,7 @@
             pltpu.VMEM((tokens, HEAD_DIM), bf16),
             pltpu.VMEM((shards, slots, HEAD_DIM), bf16),
             pltpu.SemaphoreType.DMA((3,)),
+            pltpu.SemaphoreType.REGULAR((2,)),
             pltpu.SemaphoreType.DMA((7,)),
             pltpu.SemaphoreType.DMA((7,)),
         ],

time: 115 us -> 114 us (level)
    pallas_call x1, Pallas kernels: 113 us -> 112 us  [per_device(): pl.pallas_call(functools.partial(kernel, shards), name='attention', out_s...]
where the time goes in v4:
time: 114 us
  Pallas kernels  113 us (99%)
  between operations  1.31 us (1%)
    pallas_call x1, Pallas kernels, per_device(): pl.pallas_call(functools.partial(kernel, shards), name='attention', out_s...  112 us

profile of v4, /device:TPU:62, one launch (start us, length us, event | category | flops | bytes accessed | tf_op | source)
XLA Modules:
  0.0 114.2 jit_solution(17349971600434858794)
XLA Ops:
  0.6 0.0 copy-start
  1.3 0.0 copy-done
  1.3 111.9 %attention.1 = (bf16[96,4096]{1,0:T(8,128)(2,1)S(1)}, bf16[48,4096]{1,0:T(8,128)(2,1)S(1)}) custom-call(bf16[96,4096]{1,0:T(8,128)(2,1)} %q_ref.1, bf16[96,4096]{1,0:T(8,128)(2,1)} %k_ref.1, bf16[96,4096]{1,0:T(8,128)(2,1)} %v_ref.1, bf16[96,4096]{1,0:T(8,128)(2,1)} %fq_ref.1, bf16[96,4096]{1,0:T(8,128)(2,1)} %fk_ref.1, bf16[96,4096]{1,0:T(8,128)(2,1)} %fv_ref.1, ...), custom_call_target="tpu_custom_call" | custom-call | flops 7247757312 | bytes 4718592 | tf_op jit(solution)/shard_map/attention/pallas_call | solution.py:317
  113.2 1.0 hand_over.1
Async XLA Ops:
  0.6 0.7 copy-start

commit v5 on v4

--- a/solution.py
+++ b/solution.py
@@ -10,7 +10,7 @@
 
 HEAD_DIM = 128
 PLANES = 8
-VMEM_LIMIT = 105 * 2**19
+VMEM_LIMIT = 40 * 2**20
 MESH = pl.DeviceIdType.MESH
 KEY_CHUNK = 256
 EXP2_SCALE = math.log2(math.e) / math.sqrt(HEAD_DIM)
@@ -51,6 +51,7 @@
     q_buf,
     k_buf,
     v_buf,
+    rows_own,
     fresh_own,
     fresh_out,
     fresh_buf,
@@ -110,6 +111,7 @@
         pltpu.make_async_copy(ref, fresh_own.at[i], load_sem.at[i])
         for i, ref in enumerate((fq_ref, fk_ref, fv_ref))
     ]
+    loads.append(pltpu.make_async_copy(rows_ref, rows_own, load_sem.at[3]))
     for load in loads:
         load.start()
 
@@ -159,17 +161,15 @@
             ref.at[:, columns(me)], buf.at[rows_of(me), pl.ds(0, HEAD_DIM)], recv_sem.at[n]
         ).start()
 
+    for load in loads:
+        load.wait()
     count = count_ref[0]
     lane = lax.broadcasted_iota(jnp.int32, (1, slots), 1)
-    listed = jnp.zeros((1, slots), jnp.int32)
-    for j in range(slots):
-        listed = jnp.where(lane == j, rows_ref[0, j], listed)
+    listed = rows_own[...]
     list_out[...] = jnp.full(list_out.shape, count, jnp.int32)
     list_out[0:1, 0:slots] = jnp.where(lane < count, listed, -1)
     pick = (lax.broadcasted_iota(jnp.int32, (own, slots), 0) == listed).astype(jnp.float32)
     pick = jnp.transpose(pick).astype(jnp.bfloat16)
-    for load in loads:
-        load.wait()
 
     def gather(head, carry):
         for i in range(3):
@@ -225,17 +225,35 @@
         def _():
             pltpu.make_async_copy(src, dst, recv_sem.at[n]).start()
 
+    eager = lax.rem(lax.axis_index("doc"), 2) == 0
+
+    def send_refresh(first):
+        for j in range(width):
+            to = first + j
+            send_home(refresh_buf.at[rows_of(to)], refresh_ref.at[:, columns(me)], to, 5)
+
     def refresh(i, carry):
         first = plane(i) * width
         block = pl.ds(pl.multiple_of(first * own, width * own), width * own)
         out = attend(q_buf[block, :], k_buf, v_buf)
         refresh_buf[block, :] = out.astype(jnp.bfloat16)
-        for j in range(width):
-            to = first + j
-            send_home(refresh_buf.at[rows_of(to)], refresh_ref.at[:, columns(me)], to, 5)
+
+        @pl.when(eager)
+        def _():
+            send_refresh(first)
+
         return carry
 
     lax.fori_loop(0, PLANES, refresh, 0)
+
+    @pl.when(jnp.logical_not(eager))
+    def _():
+        def late(i, carry):
+            send_refresh(plane(i) * width)
+            return carry
+
+        lax.fori_loop(0, PLANES, late, 0)
+
 
     arrived(fresh_buf, 3)
     arrived(list_buf, 4)
@@ -314,6 +332,18 @@
     bf16 = jnp.bfloat16
     hbm = pl.BlockSpec(memory_space=pltpu.HBM)
     anywhere = pl.BlockSpec(memory_space=pl.ANY)
+    operands = [
+        pltpu.with_memory_space_constraint(operand, pltpu.HBM)
+        for operand in (
+            queries,
+            keys,
+            values,
+            fresh_queries,
+            fresh_keys,
+            fresh_values,
+            masked_rows,
+        )
+    ]
     results = pl.pallas_call(
         functools.partial(kernel, shards),
         name="attention",
@@ -321,12 +351,13 @@
             jax.ShapeDtypeStruct((own, width), bf16),
             jax.ShapeDtypeStruct((slots, width), bf16),
         ),
-        in_specs=[hbm] * 6 + [pl.BlockSpec(memory_space=pltpu.SMEM)] * 2,
+        in_specs=[hbm] * 7 + [pl.BlockSpec(memory_space=pltpu.SMEM)],
         out_specs=(anywhere, anywhere),
         scratch_shapes=[
             pltpu.VMEM((tokens, HEAD_DIM), bf16),
             pltpu.VMEM((tokens, HEAD_DIM), bf16),
             pltpu.VMEM((tokens, 2 * HEAD_DIM), bf16),
+            pltpu.VMEM((1, slots), jnp.int32),
             pltpu.VMEM((3, own, width), bf16),
             pltpu.VMEM((shards, slots, 3 * HEAD_DIM), bf16),
             pltpu.VMEM((shards, slots, 3 * HEAD_DIM), bf16),
@@ -334,7 +365,7 @@
             pltpu.VMEM((shards, 1, HEAD_DIM), jnp.int32),
             pltpu.VMEM((tokens, HEAD_DIM), bf16),
             pltpu.VMEM((shards, slots, HEAD_DIM), bf16),
-            pltpu.SemaphoreType.DMA((3,)),
+            pltpu.SemaphoreType.DMA((4,)),
             pltpu.SemaphoreType.REGULAR((2,)),
             pltpu.SemaphoreType.DMA((7,)),
             pltpu.SemaphoreType.DMA((7,)),
@@ -348,13 +379,7 @@
             transcendentals=tokens * tokens * 3 // 2,
         ),
     )(
-        queries,
-        keys,
-        values,
-        fresh_queries,
-        fresh_keys,
-        fresh_values,
-        masked_rows,
+        *operands,
         masked_counts,
     )
     return pl.pallas_call(

time: 114 us -> 114 us (level)
  no operation moved by 1% of the time
where the time goes in v5:
time: 114 us
  Pallas kernels  112 us (98%)
  between operations  1.29 us (1%)
    pallas_call x1, Pallas kernels, per_device(): pl.pallas_call(functools.partial(kernel, shards), name='attention', out_s...  111 us

profile of v5, /device:TPU:62, one launch (start us, length us, event | category | flops | bytes accessed | tf_op | source)
XLA Modules:
  0.0 113.6 jit_solution(6015658517876011295)
XLA Ops:
  1.3 111.3 %attention.1 = (bf16[96,4096]{1,0:T(8,128)(2,1)S(1)}, bf16[48,4096]{1,0:T(8,128)(2,1)S(1)}) custom-call(bf16[96,4096]{1,0:T(8,128)(2,1)} %q_ref.1, bf16[96,4096]{1,0:T(8,128)(2,1)} %k_ref.1, bf16[96,4096]{1,0:T(8,128)(2,1)} %v_ref.1, bf16[96,4096]{1,0:T(8,128)(2,1)} %fq_ref.1, bf16[96,4096]{1,0:T(8,128)(2,1)} %fk_ref.1, bf16[96,4096]{1,0:T(8,128)(2,1)} %fv_ref.1, ...), custom_call_target="tpu_custom_call" | custom-call | flops 7247757312 | bytes 4718592 | tf_op jit(solution)/shard_map/attention/pallas_call | solution.py:347
  112.6 1.0 hand_over.1

commit v6 on v5

--- a/solution.py
+++ b/solution.py
@@ -246,17 +246,21 @@
 
     lax.fori_loop(0, PLANES, refresh, 0)
 
-    @pl.when(jnp.logical_not(eager))
-    def _():
-        def late(i, carry):
-            send_refresh(plane(i) * width)
-            return carry
-
-        lax.fori_loop(0, PLANES, late, 0)
+    def send_late(begin, end):
+        @pl.when(jnp.logical_not(eager))
+        def _():
+            def late(i, carry):
+                send_refresh(plane(i) * width)
+                return carry
+
+            lax.fori_loop(begin, end, late, 0)
+
+    send_late(0, 1)
 
 
     arrived(fresh_buf, 3)
     arrived(list_buf, 4)
+    send_late(1, PLANES)
 
     def update(i, carry):
         for j in range(width):

time: 114 us -> 114 us (level)
  no operation moved by 1% of the time
where the time goes in v6:
time: 114 us
  Pallas kernels  112 us (98%)
  between operations  1.29 us (1%)
    pallas_call x1, Pallas kernels, per_device(): pl.pallas_call(functools.partial(kernel, shards), name='attention', out_s...  111 us

profile of v6, /device:TPU:62, one launch (start us, length us, event | category | flops | bytes accessed | tf_op | source)
XLA Modules:
  0.0 113.6 jit_solution(13103512851538105557)
XLA Ops:
  1.3 111.3 %attention.1 = (bf16[96,4096]{1,0:T(8,128)(2,1)S(1)}, bf16[48,4096]{1,0:T(8,128)(2,1)S(1)}) custom-call(bf16[96,4096]{1,0:T(8,128)(2,1)} %q_ref.1, bf16[96,4096]{1,0:T(8,128)(2,1)} %k_ref.1, bf16[96,4096]{1,0:T(8,128)(2,1)} %v_ref.1, bf16[96,4096]{1,0:T(8,128)(2,1)} %fq_ref.1, bf16[96,4096]{1,0:T(8,128)(2,1)} %fk_ref.1, bf16[96,4096]{1,0:T(8,128)(2,1)} %fv_ref.1, ...), custom_call_target="tpu_custom_call" | custom-call | flops 7247757312 | bytes 4718592 | tf_op jit(solution)/shard_map/attention/pallas_call | solution.py:351
  112.6 1.0 hand_over.1

commit v7 on v5

--- a/solution.py
+++ b/solution.py
@@ -104,7 +104,8 @@
     plane_mates = [(0, dx) for dx in range(1, width)]
     column_far, column_near = [(2, 0), (PLANES - 2, 0)], [(1, 0), (PLANES - 1, 0)]
     barrier = pltpu.get_barrier_semaphore()
-    for place in column_far + column_near + plane_mates:
+    column_most = [(PLANES // 2, 0), (PLANES // 2 - 1, 0), (PLANES // 2 + 1, 0)]
+    for place in column_most + column_far + column_near + plane_mates:
         signal(barrier, *place)
 
     loads = [
@@ -139,17 +140,14 @@
     near = column_far + column_near
     far = [(PLANES // 2, 0), (PLANES // 2 - 1, 0), (PLANES // 2 + 1, 0)]
 
-    pl.semaphore_wait(barrier, len(near) + len(plane_mates))
-    for place in column_far + plane_mates:
+    pl.semaphore_wait(barrier, len(far) + len(near) + len(plane_mates))
+    for place in plane_mates:
         signal(ready_sem.at[0], *place)
+    send_a(0, far, own_column)
     send_a(0, near, own_column)
     send_a(1, near, own_column)
-    pl.semaphore_wait(ready_sem.at[0], len(column_far) + len(plane_mates))
-    for place in plane_mates:
-        signal(ready_sem.at[1], *place)
-    send_a(0, far, own_column)
+    pl.semaphore_wait(ready_sem.at[0], len(plane_mates))
     send_a(0, near, other_columns)
-    pl.semaphore_wait(ready_sem.at[1], len(plane_mates))
     send_a(0, far, other_columns)
     send_a(1, far, own_column)
     send_a(1, far + near, other_columns)
@@ -366,7 +364,7 @@
             pltpu.VMEM((tokens, HEAD_DIM), bf16),
             pltpu.VMEM((shards, slots, HEAD_DIM), bf16),
             pltpu.SemaphoreType.DMA((4,)),
-            pltpu.SemaphoreType.REGULAR((2,)),
+            pltpu.SemaphoreType.REGULAR((1,)),
             pltpu.SemaphoreType.DMA((7,)),
             pltpu.SemaphoreType.DMA((7,)),
         ],

time: 114 us -> 114 us (level)
  no operation moved by 1% of the time
where the time goes in v7:
time: 114 us
  Pallas kernels  112 us (98%)
  between operations  1.29 us (1%)
    pallas_call x1, Pallas kernels, per_device(): pl.pallas_call(functools.partial(kernel, shards), name='attention', out_s...  111 us

profile of v7, /device:TPU:62, one launch (start us, length us, event | category | flops | bytes accessed | tf_op | source)
XLA Modules:
  0.0 113.6 jit_solution(1207542649641314677)
XLA Ops:
  1.3 111.3 %attention.1 = (bf16[96,4096]{1,0:T(8,128)(2,1)S(1)}, bf16[48,4096]{1,0:T(8,128)(2,1)S(1)}) custom-call(bf16[96,4096]{1,0:T(8,128)(2,1)} %q_ref.1, bf16[96,4096]{1,0:T(8,128)(2,1)} %k_ref.1, bf16[96,4096]{1,0:T(8,128)(2,1)} %v_ref.1, bf16[96,4096]{1,0:T(8,128)(2,1)} %fq_ref.1, bf16[96,4096]{1,0:T(8,128)(2,1)} %fk_ref.1, bf16[96,4096]{1,0:T(8,128)(2,1)} %fv_ref.1, ...), custom_call_target="tpu_custom_call" | custom-call | flops 7247757312 | bytes 4718592 | tf_op jit(solution)/shard_map/attention/pallas_call | solution.py:345
  112.6 1.0 hand_over.1
